TPU v7x, 128 devices: a whole 4x4x4 slice. The times are simulated.
128 devices in a mesh: island: 4 (over x_lo, core), fsdp: 32 (over x_hi, z, y).
Axes of the slice: x: 4 (x_hi: 2, x_lo: 2; x = x_hi * 2 + x_lo), y: 4, z: 4, core: 2. Of those that a mesh axis runs over, the one named last changes fastest.
Arguments:
- tokens: bfloat16 [4, 512, 4096], P('island', 'fsdp'), may hold values from -6 to 6
- w_gate: bfloat16 [4, 4096, 28672], P('island', None, 'fsdp'), may hold values from -6 to 6
- w_up: bfloat16 [4, 4096, 28672], P('island', None, 'fsdp'), may hold values from -6 to 6
- d_hidden: bfloat16 [4, 512, 28672], P('island', None, 'fsdp'), may hold values from -6 to 6
- outer_rows: float32 [2, 128, 28672], P(None, None, 'fsdp'), may hold values from -6 to 6
- outer_momentum: float32 [2, 128, 28672], P(None, None, 'fsdp'), may hold values from -4 to 4
- adam_first: float32 [4, 2, 128, 28672], P('island', None, None, 'fsdp'), may hold values from -3 to 3
- adam_second: float32 [4, 2, 128, 28672], P('island', None, None, 'fsdp'), may hold values from 0.04 to 1
- fragment_rows: int32 [128], replicated, may hold values from 0 to 4095, as said below
Outputs:
- d_tokens: bfloat16 [4, 512, 4096], P('island', 'fsdp')
- fragment_weights: bfloat16 [4, 2, 128, 28672], P('island', None, None, 'fsdp')
- outer_new: float32 [2, 128, 28672], P(None, None, 'fsdp')
- momentum_new: float32 [2, 128, 28672], P(None, None, 'fsdp')
- first_new: float32 [4, 2, 128, 28672], P('island', None, None, 'fsdp')
- second_new: float32 [4, 2, 128, 28672], P('island', None, None, 'fsdp')
Inputs may be any that keep to these rules, and one draw needn't show every extreme that they name: `fragment_rows`: distinct row numbers.
All inputs are finite; a program needn't handle non-finite values.
Results may differ from a plain program's by a relative error of at most 0.005.
Values may be sent and summed in bfloat16 or wider, within the bound.
A program may use at most 128 MiB of HBM per device.

v0:
```python
import jax
import jax.numpy as jnp
from jax import lax
from jax.sharding import PartitionSpec as P


def silu_parts(gate_pre):
    sigmoid_val = jax.nn.sigmoid(gate_pre)
    return (gate_pre * sigmoid_val, sigmoid_val * (1.0 + gate_pre * (1.0 - sigmoid_val)))


def outer_step(mean_delta, outer_part, momentum_part):
    momentum_next = 0.9 * momentum_part + mean_delta
    return (outer_part - 0.7 * (mean_delta + 0.9 * momentum_next), momentum_next)


def per_device(
    tokens,
    w_gate,
    w_up,
    d_hidden,
    outer_rows,
    outer_momentum,
    adam_first,
    adam_second,
    fragment_rows,
):
    factor = float(tokens.shape[2]) ** (-0.5)
    gate_weights = w_gate[0]
    up_weights = w_up[0]
    gathered = lax.all_gather(tokens[0], "fsdp", axis=0, tiled=True)
    gate_pre = jnp.dot(gathered, gate_weights, preferred_element_type=jnp.float32) * factor
    up_pre = jnp.dot(gathered, up_weights, preferred_element_type=jnp.float32) * factor
    silu_value, silu_slope = silu_parts(gate_pre)
    upstream = d_hidden[0].astype(jnp.float32)
    d_gate = (upstream * up_pre * silu_slope).astype(jnp.bfloat16)
    d_up = (upstream * silu_value).astype(jnp.bfloat16)
    contract = (((1,), (1,)), ((), ()))

    def one_term(cotangent, weights):
        return lax.dot_general(cotangent, weights, contract, preferred_element_type=jnp.float32)

    gate_share = lax.psum_scatter(
        one_term(d_gate, gate_weights), "fsdp", scatter_dimension=0, tiled=True
    )
    up_share = lax.psum_scatter(one_term(d_up, up_weights), "fsdp", scatter_dimension=0, tiled=True)
    input_grad = gate_share + up_share
    d_tokens = (input_grad * factor).astype(jnp.bfloat16)[None]
    picked = jnp.take(gathered, fragment_rows, axis=1)
    over_tokens = (((0,), (0,)), ((), ()))
    gradient = (
        jnp.stack(
            [
                lax.dot_general(picked, d_gate, over_tokens, preferred_element_type=jnp.float32),
                lax.dot_general(picked, d_up, over_tokens, preferred_element_type=jnp.float32),
            ]
        )
        * factor
    )
    island_rows = jnp.stack(
        [jnp.take(gate_weights, fragment_rows, axis=0), jnp.take(up_weights, fragment_rows, axis=0)]
    ).astype(jnp.float32)
    pseudo = outer_rows - island_rows
    island_count = lax.axis_size("island")
    summed_delta = lax.psum(pseudo, "island")
    outer_new, momentum_new = outer_step(
        summed_delta / float(island_count), outer_rows, outer_momentum
    )
    first_new = 0.9 * adam_first + 0.1 * gradient[None]
    second_new = 0.95 * adam_second + 0.05 * (gradient * gradient)[None]
    weights_new = outer_new[None] * (1.0 - 0.02 * 0.1) - 0.02 * first_new / (
        jnp.sqrt(second_new) + 1e-08
    )
    return (
        d_tokens,
        weights_new.astype(jnp.bfloat16),
        outer_new,
        momentum_new,
        first_new,
        second_new,
    )


def solution(mesh):
    return jax.shard_map(
        per_device,
        mesh=mesh,
        in_specs=(
            P("island", "fsdp", None),
            P("island", None, "fsdp"),
            P("island", None, "fsdp"),
            P("island", None, "fsdp"),
            P(None, None, "fsdp"),
            P(None, None, "fsdp"),
            P("island", None, None, "fsdp"),
            P("island", None, None, "fsdp"),
            P(),
        ),
        out_specs=(
            P("island", "fsdp", None),
            P("island", None, None, "fsdp"),
            P(None, None, "fsdp"),
            P(None, None, "fsdp"),
            P("island", None, None, "fsdp"),
            P("island", None, None, "fsdp"),
        ),
        check_vma=False,
    )
```

profile of v0, /device:TPU:0, one launch (start us, length us, event | category | flops | bytes accessed | tf_op | source)
XLA Modules:
  0.0 340.5 jit_solution(8726549646487029111)
XLA Ops:
  8.0 0.0 copy-start.6
  8.0 0.0 copy-start.1
  8.0 0.0 copy-start.5
  8.0 0.0 all-gather.3.cloned.1.call-start
  8.1 0.7 all-gather.3.cloned.1.call-update
  8.8 0.0 all-reduce.2.cloned.1.call-start
  8.8 0.7 compare_select_fusion
  9.5 5.0 %gather_fusion.2 = bf16[128,896]{1,0:T(8,128)(2,1)S(1)} fusion(bf16[4096,896]{1,0:T(8,128)(2,1)} %bitcast.49, s32[1024]{0:T(1024)S(1)} %pad_clamp_fusion), kind=kCustom, calls=%fused_computation.1.clone | custom fusion | bytes 459264 | tf_op jit(solution)/shard_map/jit(_take)/gather | solution.py:61
  14.5 5.0 %gather_fusion.1 = bf16[128,896]{1,0:T(8,128)(2,1)S(1)} fusion(bf16[4096,896]{1,0:T(8,128)(2,1)} %bitcast.46, s32[1024]{0:T(1024)S(1)} %pad_clamp_fusion), kind=kCustom, calls=%fused_computation.clone | custom fusion | bytes 459264 | tf_op jit(solution)/shard_map/jit(_take)/gather | solution.py:61
  19.6 0.0 copy-done.6
  19.6 0.1 select_bitcast_fusion.1
  19.7 0.0 copy-done.1
  19.7 1.0 convert_subtract_fusion
  20.7 0.0 all-reduce.2.cloned.1.call-update
  20.8 0.2 reduce-scatter.2.cloned.1.call-start
  21.0 74.0 %all-gather.3.cloned.1.call-done = bf16[1,512,4096]{2,1,0:T(8,128)(2,1)} async-done(((bf16[1,16,4096]{2,1,0:T(8,128)(2,1)}), bf16[1,512,4096]{2,1,0:T(8,128)(2,1)}) %all-gather.3.cloned.1.call-update) | async-done | bytes 4194320 | tf_op jit(solution)/shard_map/all_gather | solution.py:31
  95.0 0.0 copy-done.5
  95.0 0.0 copy-start
  95.0 0.0 slice-start
  95.0 0.0 slice-start.2
  95.0 10.4 %fusion.6 = (bf16[512,896]{1,0:T(8,128)(2,1)S(1)}, f32[512,896]{1,0:T(8,128)S(1)}) fusion(bf16[1,512,896]{2,1,0:T(8,128)(2,1)S(1)} %copy-done.5, bf16[1,4096,896]{2,1,0:T(8,128)(2,1)} %param.12, bf16[1,512,4096]{2,1,0:T(8,128)(2,1)} %all-gather.3.cloned.1.call-done), kind=kOutput, calls=%fused_computation.12 | convolution fusion | flops 3761766400 | bytes 15204352 | tf_op jit(solution)/shard_map/dot_general | solution.py:32
  105.4 0.0 copy-start.3
  105.4 0.0 copy-done
  105.4 0.0 slice-start.1
  105.4 0.0 slice-start.3
  105.4 8.4 %fusion.5 = bf16[512,896]{1,0:T(8,128)(2,1)S(1)} fusion(f32[512,896]{1,0:T(8,128)S(1)} %get-tuple-element.15, bf16[1,512,4096]{2,1,0:T(8,128)(2,1)S(1)} %copy-done, bf16[1,512,896]{2,1,0:T(8,128)(2,1)S(1)} %copy-done.5, bf16[1,4096,896]{2,1,0:T(8,128)(2,1)} %param.13), kind=kOutput, calls=%fused_computation.11 | convolution fusion | flops 3764060160 | bytes 15204352 | tf_op jit(solution)/shard_map/dot_general | solution.py:33
  113.8 0.0 slice-done
  113.9 0.0 slice-done.1
  113.9 0.0 copy-start.4
  113.9 6.7 %fusion.11 = f32[512,4096]{1,0:T(8,128)} fusion(bf16[512,896]{1,0:T(8,128)(2,1)S(1)} %fusion.5, bf16[1,4096,896]{2,1,0:T(8,128)(2,1)S(1)} %bitcast.48), kind=kOutput, calls=%fused_computation.32 | convolution fusion | flops 3758096384 | bytes 16646144 | tf_op jit(solution)/shard_map/dot_general | solution.py:41
  120.6 0.0 copy-done.4
  120.6 0.0 copy-done.3
  120.6 0.0 slice-done.2
  120.6 0.0 slice-done.3
  120.6 9.0 %convolution_add_fusion = f32[512,4096]{1,0:T(8,128)} fusion(f32[512,4096]{1,0:T(8,128)} %fusion.11, bf16[512,896]{1,0:T(8,128)(2,1)S(1)} %get-tuple-element.14, bf16[1,4096,896]{2,1,0:T(8,128)(2,1)S(1)} %bitcast.51), kind=kOutput, calls=%fused_computation.3 | convolution fusion | flops 3760193536 | bytes 25034752 | tf_op jit(solution)/shard_map/dot_general | solution.py:41
  129.6 0.0 reduce-scatter.2.cloned.1.call-update
  129.6 6.5 %copy.16 = bf16[1,512,4096]{1,2,0:T(8,128)(2,1)} copy(bf16[1,512,4096]{2,1,0:T(8,128)(2,1)} %all-gather.3.cloned.1.call-done) | data formatting | bytes 8388608 | tf_op jit(solution)/shard_map/all_gather | solution.py:31
  136.1 0.0 copy-start.2
  136.1 3.9 %gather_fusion = bf16[128,512]{1,0:T(8,128)(2,1)S(1)} fusion(bf16[512,4096]{0,1:T(8,128)(2,1)} %bitcast.45, s32[1024]{0:T(1024)S(1)} %pad_clamp_fusion), kind=kCustom, calls=%fused_computation.2 | custom fusion | bytes 262656 | tf_op jit(solution)/shard_map/jit(_take)/gather | solution.py:49
  140.0 1.5 convolution_bitcast_fusion.1
  141.5 1.5 convolution_bitcast_fusion
  143.1 0.0 all-reduce.2.cloned.1.call-done
  143.1 0.0 copy-done.2
  143.1 4.0 %fusion.9 = (bf16[1,2,128,896]{3,2,1,0:T(8,128)(2,1)}, f32[2,128,896]{2,1,0:T(8,128)}, f32[2,128,896]{2,1,0:T(8,128)}, f32[1,2,128,896]{3,2,1,0:T(8,128)}, f32[1,2,128,896]{3,2,1,0:T(8,128)}) fusion(f32[2,128,896]{2,1,0:T(8,128)S(1)} %copy-done.1, f32[2,128,896]{2,1,0:T(8,128)} %all-reduce.2.cloned.1.call-done, f32[2,128,896]{2,1,0:T(8,128)S(1)} %copy-done.2, ...), kind=kLoop, calls=%fused_computation.18 | loop fusion | flops 5046272 | bytes 9633792 | tf_op jit(solution)/shard_map/convert_element_type | solution.py:76
  147.1 184.3 %reduce-scatter.2.cloned.1.call-done = f32[16,4096]{1,0:T(8,128)} async-done(((f32[512,4096]{1,0:T(8,128)}), f32[16,4096]{1,0:T(8,128)}) %reduce-scatter.2.cloned.1.call-update) | async-done | bytes 262160 | tf_op jit(solution)/shard_map/reduce_scatter | solution.py:43
  331.4 1.6 fusion.10
  (4 shorter events, 0.0 us)
Async XLA Ops:
  8.0 11.6 %copy-start.6 = (s32[128]{0:T(128)S(1)}, s32[128]{0:T(128)}, u32[]{:S(2)}) copy-start(s32[128]{0:T(128)} %param.19) | copy-start | bytes 1540
  8.0 11.7 %copy-start.1 = (f32[2,128,896]{2,1,0:T(8,128)S(1)}, f32[2,128,896]{2,1,0:T(8,128)}, u32[]{:S(2)}) copy-start(f32[2,128,896]{2,1,0:T(8,128)} %param.15) | copy-start | bytes 2752516
  8.0 86.9 %copy-start.5 = (bf16[1,512,896]{2,1,0:T(8,128)(2,1)S(1)}, bf16[1,512,896]{2,1,0:T(8,128)(2,1)}, u32[]{:S(2)}) copy-start(bf16[1,512,896]{2,1,0:T(8,128)(2,1)} %param.14) | copy-start | bytes 2752516
  8.0 86.9 %all-gather.3.cloned.1.call-start = ((), (), s32[]{:S(2)}) async-start(), calls=%async_computation.2 | async-start | bytes 4325376 | tf_op jit(solution)/shard_map/all_gather | solution.py:31
  8.8 134.3 %all-reduce.2.cloned.1.call-start = ((), (), s32[]{:S(2)}) async-start(), calls=%async_computation.1 | async-start | bytes 1835008 | tf_op jit(solution)/shard_map/psum | solution.py:65
  20.8 310.6 %reduce-scatter.2.cloned.1.call-start = ((), (), s32[]{:S(2)}) async-start(), calls=%async_computation.3 | async-start | bytes 8650752 | tf_op jit(solution)/shard_map/reduce_scatter | solution.py:43
  95.0 10.4 %copy-start = (bf16[1,512,4096]{2,1,0:T(8,128)(2,1)S(1)}, bf16[1,512,4096]{2,1,0:T(8,128)(2,1)}, u32[]{:S(2)}) copy-start(bf16[1,512,4096]{2,1,0:T(8,128)(2,1)} %all-gather.3.cloned.1.call-done) | copy-start | bytes 12582916
  95.0 18.9 %slice-start = ((s8[7340032]{0:T(1024)(128)(4,1)}), s8[4194304]{0:T(1024)(128)(4,1)S(1)}, s32[]{:S(2)}) async-start(s8[7340032]{0:T(1024)(128)(4,1)} %bitcast.47), calls=%async_computation.4 | async-start | bytes 8388608
  95.0 25.6 %slice-start.2 = ((s8[7340032]{0:T(1024)(128)(4,1)}), s8[4194304]{0:T(1024)(128)(4,1)S(1)}, s32[]{:S(2)}) async-start(s8[7340032]{0:T(1024)(128)(4,1)} %bitcast.50), calls=%async_computation.6 | async-start | bytes 8388608
  105.4 15.2 %copy-start.3 = (bf16[512,896]{1,0:T(8,128)(2,1)}, bf16[512,896]{1,0:T(8,128)(2,1)S(1)}, u32[]{:S(2)}) copy-start(bf16[512,896]{1,0:T(8,128)(2,1)S(1)} %get-tuple-element.14) | copy-start | bytes 2752516
  105.4 8.5 %slice-start.1 = ((s8[7340032]{0:T(1024)(128)(4,1)}), s8[3145728]{0:T(1024)(128)(4,1)S(1)}, s32[]{:S(2)}) async-start(s8[7340032]{0:T(1024)(128)(4,1)} %bitcast.47), calls=%async_computation.5 | async-start | bytes 6291456
  105.4 15.2 %slice-start.3 = ((s8[7340032]{0:T(1024)(128)(4,1)}), s8[3145728]{0:T(1024)(128)(4,1)S(1)}, s32[]{:S(2)}) async-start(s8[7340032]{0:T(1024)(128)(4,1)} %bitcast.50), calls=%async_computation.7 | async-start | bytes 6291456
  113.9 6.7 %copy-start.4 = (bf16[512,896]{1,0:T(8,128)(2,1)}, bf16[512,896]{1,0:T(8,128)(2,1)S(1)}, u32[]{:S(2)}) copy-start(bf16[512,896]{1,0:T(8,128)(2,1)S(1)} %fusion.5) | copy-start | bytes 2752516
  136.1 7.0 %copy-start.2 = (f32[2,128,896]{2,1,0:T(8,128)S(1)}, f32[2,128,896]{2,1,0:T(8,128)}, u32[]{:S(2)}) copy-start(f32[2,128,896]{2,1,0:T(8,128)} %param.16) | copy-start | bytes 2752516
Sparse Core Ops, SparseCore 0:
  11.9 82.9 all-gather.2
  129.7 201.6 reduce-scatter.1
Sparse Core Ops, SparseCore 1:
  20.8 42.5 all-reduce.1
where the time goes:
time: 341 us; the launch traced here: 340 us
  waiting for transfers between devices  259 us (76%)
  matrix products  37.6 us (11%)
  local copies, waits for them, and re-layouts  20.5 us (6%)
  between operations  15.7 us (5%)
  other arithmetic  7.4 us (2%)
    reduce_scatter x1, waiting for transfers between devices, per_device(): lax.psum_scatter(one_term(d_gate, gate_weights), 'fsdp', scatter_dimensio...  184 us
    all_gather x1, waiting for transfers between devices, per_device(): gathered = lax.all_gather(tokens[0], 'fsdp', axis=0, tiled=True)  74 us
    dot_general x2, matrix products, one_term(): lax.dot_general(cotangent, weights, contract, preferred_element_type=jnp....  15.7 us
    dot_general x1, matrix products, per_device(): jnp.dot(gathered, gate_weights, preferred_element_type=jnp.float32) * factor  10.4 us
    dot_general x1, matrix products, per_device(): jnp.dot(gathered, up_weights, preferred_element_type=jnp.float32) * factor  8.41 us
  transfers between devices with their start and end apart: 3, of which 2 were waited for; matrix products, arithmetic and copies ran while one was open for 19% of the time, Pallas kernels for 0%

commit v1 on v0

v1 whole, which is shorter than its diff:
```python
import functools

import jax
import jax.numpy as jnp
from jax import lax
from jax.experimental import pallas as pl
from jax.experimental.pallas import tpu as pltpu
from jax.sharding import PartitionSpec as P

MESH = pl.DeviceIdType.MESH
BF = jnp.bfloat16
F32 = jnp.float32

D = 4096
HID = 896
W2 = 2 * HID
TOK = 512
OWN = 16
FRAG = 128
NP = 4
NC = 2 * NP
DC = D // NC
HC = DC // 2
PC = 2 * DC
FACTOR = float(D) ** (-0.5)

AG = 9
RS = 9


def step_kernel(
    tok_hbm, wg_hbm, wu_hbm, dh_hbm, row_ref, col_ref,
    dtok_hbm, grad_hbm, rsum_hbm,
    wts, toks, acc, dcat, dhid, part, oh, oht, pick, rowp, rows_all, gradv, rsumv, dtokv,
    sb1, rb1, sb2, rb2, quart, last, sbx, rbx,
    w_sem, l_sem, o_sem, ag_s, ag_r, rs_s, rs_r, is_s, is_r,
):
    isl = lax.axis_index("island")
    f = lax.axis_index("fsdp")
    x = f // 16
    z = (f // 4) % 4
    y = f % 4
    xl = isl // 2
    core = isl % 2

    def at(xx, zz, yy):
        return (isl, xx * 16 + zz * 4 + yy)

    up = lambda m: (m + 1) % 4
    down = lambda m: (m + 3) % 4
    opposite = lambda m: (m + 2) % 4
    ydev = (at(x, z, up(y)), at(x, z, down(y)))
    zdev = (at(x, up(z), y), at(x, down(z), y))
    xdev = at(1 - x, z, y)
    isl_core = xl * 2 + (1 - core)
    isl_x = (1 - xl) * 2 + core
    isl_far = 3 - isl
    cdev = (isl_core, f)
    ldev = (isl_x, f)

    own_copy = pltpu.make_async_copy(
        tok_hbm.at[0], toks.at[x, z, pl.ds(pl.multiple_of(y * OWN, OWN), OWN), :], l_sem.at[0]
    )
    own_copy.start()
    w_copies = []
    for p in range(NP):
        rows = pl.ds(p * PC, PC)
        pair = []
        for j, src in enumerate((wg_hbm, wu_hbm)):
            copy = pltpu.make_async_copy(
                src.at[0, rows, :], wts.at[rows, pl.ds(j * HID, HID)], w_sem.at[p, j]
            )
            copy.start()
            pair.append(copy)
        w_copies.append(pair)
    dh_copy = pltpu.make_async_copy(dh_hbm.at[0], dhid, l_sem.at[1])
    dh_copy.start()

    barrier = pltpu.get_barrier_semaphore()
    for dev in (*ydev, *zdev, xdev, cdev, ldev):
        pl.semaphore_signal(barrier, inc=1, device_id=dev, device_id_type=MESH)

    def hot(p, _):
        lo = pl.multiple_of(p * 256, 256)
        down_rows = lax.broadcasted_iota(jnp.int32, (256, FRAG), 0) + lo
        oh[pl.ds(lo, 256), :] = jnp.where(down_rows == row_ref[...], 1.0, 0.0).astype(BF)
        along = lax.broadcasted_iota(jnp.int32, (FRAG, 256), 1) + lo
        oht[:, pl.ds(lo, 256)] = jnp.where(along == col_ref[...], 1.0, 0.0).astype(BF)
        return 0

    lax.fori_loop(0, D // 256, hot, 0)
    pl.semaphore_wait(barrier, 7)

    started = []

    def send(src, dst, ss, rs, dev):
        copy = pltpu.make_async_remote_copy(
            src_ref=src, dst_ref=dst, send_sem=ss, recv_sem=rs, device_id=dev, device_id_type=MESH
        )
        copy.start()
        started.append(copy)

    def arrived(ref, rs, ss):
        pltpu.make_async_remote_copy(
            src_ref=ref, dst_ref=ref, send_sem=ss, recv_sem=rs, device_id=xdev, device_id_type=MESH
        ).wait_recv()

    def ysl(m):
        return pl.ds(pl.multiple_of(m * OWN, OWN), OWN)

    def cols_of(c, half=None):
        if half is None:
            return pl.ds(c * DC, DC)
        return pl.ds(c * DC + half * HC, HC)

    def first_part(c, m, half=None):
        if c % 2 == 0:
            return toks.at[:, z, ysl(m), cols_of(c, half)]
        return toks.at[:, m, ysl(y), cols_of(c, half)]

    def second_part(c, m, half=None):
        if c % 2 == 0:
            return toks.at[:, m, :, cols_of(c, half)]
        return toks.at[:, :, ysl(m), cols_of(c, half)]

    def ring_send(c, part_of, m, dev, k):
        for j in range(2):
            send(part_of(c, m), part_of(c, m), ag_s.at[c, k + j], ag_r.at[c, k + j], dev[j])

    def ring_relay(c, part_of, m, dev, k):
        for j, near in enumerate((down(m), up(m))):
            arrived(part_of(c, near), ag_r.at[c, k + j], ag_s.at[c, k + j])
            piece = part_of(c, near, j)
            send(piece, piece, ag_s.at[c, k + 2 + j], ag_r.at[c, k + 2 + j], dev[j])

    def ring_end(c, part_of, m, k):
        for j in range(2):
            arrived(part_of(c, opposite(m), j), ag_r.at[c, k + 2 + j], ag_s.at[c, k + 2 + j])

    def axes(c):
        return ((y, ydev), (z, zdev)) if c % 2 == 0 else ((z, zdev), (y, ydev))

    for c in range(NC):
        send(
            tok_hbm.at[0, :, cols_of(c)],
            toks.at[x, z, ysl(y), cols_of(c)],
            ag_s.at[c, 0], ag_r.at[c, 0], xdev,
        )
    own_copy.wait()
    for c in range(NC):
        arrived(toks.at[1 - x, z, ysl(y), cols_of(c)], ag_r.at[c, 0], ag_s.at[c, 0])
        (m1, dev1), _ = axes(c)
        ring_send(c, first_part, m1, dev1, 1)

    def ncols(n):
        return pl.ds(pl.multiple_of(n * 256, 256), 256)

    def pick_rows(p):
        for copy in w_copies[p]:
            copy.wait()

        def body(n, _):
            value = jnp.dot(
                oht[:, p * PC:(p + 1) * PC], wts[pl.ds(p * PC, PC), ncols(n)],
                preferred_element_type=F32,
            )
            if p > 0:
                value = value + rowp[:, ncols(n)]
            rowp[:, ncols(n)] = value
            return 0

        lax.fori_loop(0, W2 // 256, body, 0)

    for p in range(NP):
        for c in (2 * p, 2 * p + 1):
            (m1, dev1), _ = axes(c)
            ring_relay(c, first_part, m1, dev1, 1)
        pick_rows(p)

    def forward(p):
        def body(n, _):
            value = jnp.dot(
                toks[:, :, :, p * PC:(p + 1) * PC].reshape(TOK, PC),
                wts[pl.ds(p * PC, PC), ncols(n)],
                preferred_element_type=F32,
            )
            if p > 0:
                value = value + acc[:, ncols(n)]
            acc[:, ncols(n)] = value
            return 0

        lax.fori_loop(0, W2 // 256, body, 0)
        value = jnp.dot(
            toks[:, :, :, p * PC:(p + 1) * PC].reshape(TOK, PC),
            oh[p * PC:(p + 1) * PC, :],
            preferred_element_type=F32,
        )
        if p > 0:
            value = value + pick[...]
        pick[...] = value

    for t in range(NP + 2):
        if t < NP:
            for c in (2 * t, 2 * t + 1):
                (m1, _), (m2, dev2) = axes(c)
                ring_end(c, first_part, m1, 1)
                ring_send(c, second_part, m2, dev2, 5)
        if 0 <= t - 1 < NP:
            for c in (2 * t - 2, 2 * t - 1):
                _, (m2, dev2) = axes(c)
                ring_relay(c, second_part, m2, dev2, 5)
        if t == 0:
            rows_all[isl] = rowp[...].astype(BF)
            send(rows_all.at[isl], rows_all.at[isl], is_s.at[0], is_r.at[0], cdev)
            send(rows_all.at[isl], rows_all.at[isl], is_s.at[1], is_r.at[1], ldev)
        if t >= 2:
            for c in (2 * t - 4, 2 * t - 3):
                _, (m2, _) = axes(c)
                ring_end(c, second_part, m2, 5)
            forward(t - 2)

    dh_copy.wait()

    def gated(r, _):
        rr = pl.ds(pl.multiple_of(r * 16, 16), 16)
        gate = acc[rr, 0:HID] * FACTOR
        upv = acc[rr, HID:W2] * FACTOR
        g = dhid[rr, :].astype(F32)
        s = jax.nn.sigmoid(gate)
        dcat[rr, 0:HID] = (g * upv * (s * (1.0 + gate * (1.0 - s)))).astype(BF)
        dcat[rr, HID:W2] = (g * (gate * s)).astype(BF)
        return 0

    lax.fori_loop(0, TOK // 16, gated, 0)

    def backward(c):
        for n in range(DC // 256):
            lo = c * DC + n * 256
            value = lax.dot_general(
                dcat[...], wts[pl.ds(lo, 256), :], (((1,), (1,)), ((), ())),
                preferred_element_type=F32,
            )
            part[:, :, :, lo:lo + 256] = value.reshape(2, 4, 64, 256)

    def block1(c, m, half=None):
        if c % 2 == 0:
            return part[:, m, :, cols_of(c, half)].reshape(128, DC if half is None else HC)
        return part[:, :, ysl(m), cols_of(c, half)].reshape(128, DC if half is None else HC)

    def block2(c, m, half=None):
        if half is None:
            return quart[c, :, m].reshape(32, DC)
        return quart[c, :, m, :, half * HC:(half + 1) * HC].reshape(32, HC)

    def far_out(c, block, m, dev, sb, rb, k):
        sb[c, 0] = block(c, opposite(m)).astype(BF)
        for j in range(2):
            hs = pl.ds(j * HC, HC)
            send(sb.at[c, 0, :, hs], rb.at[c, 0, :, hs], rs_s.at[c, k + j], rs_r.at[c, k + j], dev[j])

    def near_out(c, block, m, dev, sb, rb, k):
        for j, near in enumerate((up(m), down(m))):
            hs = pl.ds(j * HC, HC)
            ot = pl.ds((1 - j) * HC, HC)
            sb[c, 1 + j, :, ot] = block(c, near, 1 - j).astype(BF)
            arrived(rb.at[c, 0, :, hs], rs_r.at[c, k + j], rs_s.at[c, k + j])
            sb[c, 1 + j, :, hs] = (block(c, near, j) + rb[c, 0, :, hs].astype(F32)).astype(BF)
            send(
                sb.at[c, 1 + j], rb.at[c, 1 + j], rs_s.at[c, k + 2 + j], rs_r.at[c, k + 2 + j], dev[j]
            )

    def total(c, block, m, rb, k):
        for j in range(2):
            arrived(rb.at[c, 1 + j], rs_r.at[c, k + 2 + j], rs_s.at[c, k + 2 + j])
        return block(c, m) + (rb[c, 1].astype(F32) + rb[c, 2].astype(F32))

    def scatter_axes(c):
        return ((z, zdev), (y, ydev)) if c % 2 == 0 else ((y, ydev), (z, zdev))

    def gradient():
        pk = jnp.transpose(pick[...]).astype(BF)

        def body(n, _):
            gradv[:, ncols(n)] = (
                jnp.dot(pk, dcat[:, ncols(n)], preferred_element_type=F32) * FACTOR
            )
            return 0

        lax.fori_loop(0, W2 // 256, body, 0)

    grad_copy = pltpu.make_async_copy(gradv, grad_hbm, o_sem.at[0])
    rsum_copy = pltpu.make_async_copy(rsumv, rsum_hbm, o_sem.at[1])
    dtok_copy = pltpu.make_async_copy(dtokv, dtok_hbm, o_sem.at[2])

    for t in range(NP + 5):
        if t < NP:
            for c in (2 * t, 2 * t + 1):
                (m1, dev1), _ = scatter_axes(c)
                backward(c)
                far_out(c, block1, m1, dev1, sb1, rb1, 0)
        if 0 <= t - 1 < NP:
            for c in (2 * t - 2, 2 * t - 1):
                (m1, dev1), _ = scatter_axes(c)
                near_out(c, block1, m1, dev1, sb1, rb1, 0)
        if 0 <= t - 2 < NP:
            for c in (2 * t - 4, 2 * t - 3):
                (m1, _), (m2, dev2) = scatter_axes(c)
                quart[c] = total(c, block1, m1, rb1, 0).reshape(2, 4, OWN, DC)
                far_out(c, block2, m2, dev2, sb2, rb2, 4)
        if 0 <= t - 3 < NP:
            for c in (2 * t - 6, 2 * t - 5):
                _, (m2, dev2) = scatter_axes(c)
                near_out(c, block2, m2, dev2, sb2, rb2, 4)
        if 0 <= t - 4 < NP:
            for c in (2 * t - 8, 2 * t - 7):
                _, (m2, _) = scatter_axes(c)
                last[c] = total(c, block2, m2, rb2, 4).reshape(2, OWN, DC)
                sbx[c] = last[c, 1 - x].astype(BF)
                send(sbx.at[c], rbx.at[c], rs_s.at[c, 8], rs_r.at[c, 8], xdev)
        if t >= 5:
            for c in (2 * t - 10, 2 * t - 9):
                arrived(rbx.at[c], rs_r.at[c, 8], rs_s.at[c, 8])
                dtokv[:, cols_of(c)] = ((last[c, x] + rbx[c].astype(F32)) * FACTOR).astype(BF)
        if t == 1:
            gradient()
            grad_copy.start()
            arrived(rows_all.at[isl_x], is_r.at[1], is_s.at[1])
            send(rows_all.at[isl_x], rows_all.at[isl_x], is_s.at[2], is_r.at[2], cdev)
        if t == 2:
            arrived(rows_all.at[isl_core], is_r.at[0], is_s.at[0])
            arrived(rows_all.at[isl_far], is_r.at[2], is_s.at[2])

            def add_rows(r, _):
                rr = pl.ds(pl.multiple_of(r * 16, 16), 16)
                tot = rows_all[0, rr, :].astype(F32)
                for k in range(1, 4):
                    tot = tot + rows_all[k, rr, :].astype(F32)
                rsumv[rr, :] = tot
                return 0

            lax.fori_loop(0, FRAG // 16, add_rows, 0)
            rsum_copy.start()

    dtok_copy.start()
    for copy in started:
        copy.wait_send()
    grad_copy.wait()
    rsum_copy.wait()
    dtok_copy.wait()


def exchange(tokens, w_gate, w_up, d_hidden, fragment_rows):
    any_spec = pl.BlockSpec(memory_space=pl.ANY)
    vmem = pl.BlockSpec(memory_space=pltpu.VMEM)
    dma = pltpu.SemaphoreType.DMA
    return pl.pallas_call(
        step_kernel,
        out_shape=(
            jax.ShapeDtypeStruct((OWN, D), BF),
            jax.ShapeDtypeStruct((FRAG, W2), F32),
            jax.ShapeDtypeStruct((FRAG, W2), F32),
        ),
        in_specs=[any_spec] * 4 + [vmem] * 2,
        out_specs=(any_spec,) * 3,
        scratch_shapes=[
            pltpu.VMEM((D, W2), BF),
            pltpu.VMEM((2, 4, 64, D), BF),
            pltpu.VMEM((TOK, W2), F32),
            pltpu.VMEM((TOK, W2), BF),
            pltpu.VMEM((TOK, HID), BF),
            pltpu.VMEM((2, 4, 64, D), F32),
            pltpu.VMEM((D, FRAG), BF),
            pltpu.VMEM((FRAG, D), BF),
            pltpu.VMEM((TOK, FRAG), F32),
            pltpu.VMEM((FRAG, W2), F32),
            pltpu.VMEM((4, FRAG, W2), BF),
            pltpu.VMEM((FRAG, W2), F32),
            pltpu.VMEM((FRAG, W2), F32),
            pltpu.VMEM((OWN, D), BF),
            pltpu.VMEM((NC, 3, 128, DC), BF),
            pltpu.VMEM((NC, 3, 128, DC), BF),
            pltpu.VMEM((NC, 3, 32, DC), BF),
            pltpu.VMEM((NC, 3, 32, DC), BF),
            pltpu.VMEM((NC, 2, 4, OWN, DC), F32),
            pltpu.VMEM((NC, 2, OWN, DC), F32),
            pltpu.VMEM((NC, OWN, DC), BF),
            pltpu.VMEM((NC, OWN, DC), BF),
            dma((NP, 2)),
            dma((2,)),
            dma((3,)),
            dma((NC, AG)),
            dma((NC, AG)),
            dma((NC, RS)),
            dma((NC, RS)),
            dma((3,)),
            dma((3,)),
        ],
        compiler_params=pltpu.CompilerParams(
            collective_id=0, has_side_effects=True, vmem_limit_bytes=60 * 2**20
        ),
        cost_estimate=pl.CostEstimate(
            flops=16 * 10**9, bytes_accessed=18 * 10**6, transcendentals=TOK * HID
        ),
        name="gather_compute_scatter",
    )(tokens, w_gate, w_up, d_hidden, fragment_rows.reshape(1, FRAG), fragment_rows.reshape(FRAG, 1))


def adam_kernel(
    dtok, grad, rsum, outer, mom, first, second,
    dtok_out, frag_out, outer_out, mom_out, first_out, second_out,
):
    dtok_out[0] = dtok[...]
    g = grad[...]
    o = outer[0]
    mean_delta = o - rsum[...] * 0.25
    m = 0.9 * mom[0] + mean_delta
    on = o - 0.7 * (mean_delta + 0.9 * m)
    f = 0.9 * first[0, 0] + 0.1 * g
    s = 0.95 * second[0, 0] + 0.05 * (g * g)
    mom_out[0] = m
    outer_out[0] = on
    first_out[0, 0] = f
    second_out[0, 0] = s
    frag_out[0, 0] = (on * (1.0 - 0.02 * 0.1) - 0.02 * f / (jnp.sqrt(s) + 1e-08)).astype(BF)


def update(dtok, grad, rsum, outer, mom, first, second):
    rows = 32
    whole = pl.BlockSpec((OWN, D), lambda j, k: (0, 0))
    whole_out = pl.BlockSpec((1, OWN, D), lambda j, k: (0, 0, 0))
    flat = pl.BlockSpec((rows, HID), lambda j, k: (k, j))
    three = pl.BlockSpec((1, rows, HID), lambda j, k: (j, k, 0))
    four = pl.BlockSpec((1, 1, rows, HID), lambda j, k: (0, j, k, 0))
    return pl.pallas_call(
        adam_kernel,
        grid=(2, FRAG // rows),
        out_shape=(
            jax.ShapeDtypeStruct((1, OWN, D), BF),
            jax.ShapeDtypeStruct((1, 2, FRAG, HID), BF),
            jax.ShapeDtypeStruct((2, FRAG, HID), F32),
            jax.ShapeDtypeStruct((2, FRAG, HID), F32),
            jax.ShapeDtypeStruct((1, 2, FRAG, HID), F32),
            jax.ShapeDtypeStruct((1, 2, FRAG, HID), F32),
        ),
        in_specs=[whole, flat, flat, three, three, four, four],
        out_specs=(whole_out, four, three, three, four, four),
        name="update",
    )(dtok, grad, rsum, outer, mom, first, second)


def per_device(
    tokens, w_gate, w_up, d_hidden, outer_rows, outer_momentum, adam_first, adam_second, fragment_rows
):
    dtok, grad, rsum = exchange(tokens, w_gate, w_up, d_hidden, fragment_rows)
    return update(dtok, grad, rsum, outer_rows, outer_momentum, adam_first, adam_second)


def solution(mesh):
    return jax.shard_map(
        per_device,
        mesh=mesh,
        in_specs=(
            P("island", "fsdp", None),
            P("island", None, "fsdp"),
            P("island", None, "fsdp"),
            P("island", None, "fsdp"),
            P(None, None, "fsdp"),
            P(None, None, "fsdp"),
            P("island", None, None, "fsdp"),
            P("island", None, None, "fsdp"),
            P(),
        ),
        out_specs=(
            P("island", "fsdp", None),
            P("island", None, None, "fsdp"),
            P(None, None, "fsdp"),
            P(None, None, "fsdp"),
            P("island", None, None, "fsdp"),
            P("island", None, None, "fsdp"),
        ),
        check_vma=False,
    )
```

time: 341 us -> 96.2 us (0.28)
  waiting for transfers between devices: 259 us -> 0 us
  Pallas kernels: 0 us -> 93.8 us
  matrix products: 37.6 us -> 0 us
  local copies, waits for them, and re-layouts: 20.5 us -> 1.39 us
  between operations: 15.7 us -> 0.64 us
  other arithmetic: 7.4 us -> 0 us
    reduce_scatter x1 -> x0, waiting for transfers between devices: 184 us -> none  [per_device(): lax.psum_scatter(one_term(d_gate, gate_weights), 'fsdp', scatter_dimensio...]
    pallas_call x0 -> x2, Pallas kernels: none -> 93.8 us  [the longest x1 86.5 us: exchange(): pl.pallas_call(step_kernel, out_shape=(jax.ShapeDtypeStruct((OWN, D), BF)...]
    all_gather x1 -> x0, waiting for transfers between devices: 74 us -> none  [per_device(): gathered = lax.all_gather(tokens[0], 'fsdp', axis=0, tiled=True)]
    dot_general x6 -> x0, matrix products: 37.6 us -> none  [the longest x2 15.7 us: one_term(): lax.dot_general(cotangent, weights, contract, preferred_element_type=jnp....]
    gather x3 -> x0, local copies, waits for them, and re-layouts: 14 us -> none  [the longest x1 5.05 us: per_device(): jnp.take(gate_weights, fragment_rows, axis=0)]
    all_gather x1 -> x0, local copies, waits for them, and re-layouts: 6.47 us -> none  [per_device(): gathered = lax.all_gather(tokens[0], 'fsdp', axis=0, tiled=True)]
    convert_element_type x1 -> x0, other arithmetic: 3.97 us -> none  [per_device(): weights_new.astype(jnp.bfloat16)]
  transfers between devices with their start and end apart: 3 -> 0, of which waited for: 2 -> 0; matrix products, arithmetic and copies ran while one was open for 19% -> 0% of each run, Pallas kernels for 0% -> 0%
where the time goes in v1:
time: 96.2 us; the launch traced here: 95.8 us
  Pallas kernels  93.8 us (98%)
  local copies, waits for them, and re-layouts  1.39 us (1%)
    pallas_call x1, Pallas kernels, exchange(): pl.pallas_call(step_kernel, out_shape=(jax.ShapeDtypeStruct((OWN, D), BF)...  86.5 us
    pallas_call x1, Pallas kernels, update(): pl.pallas_call(adam_kernel, grid=(2, FRAG // rows), out_shape=(jax.ShapeD...  7.29 us

profile of v1, /device:TPU:0, one launch (start us, length us, event | category | flops | bytes accessed | tf_op | source)
XLA Modules:
  0.0 95.8 jit_solution(10962118662764456099)
XLA Ops:
  0.6 1.4 %copy.15.col_ref = s32[128,1]{1,0:T(8,128)} copy(s32[128,1]{0,1:T(1,128)} %bitcast.2) | data formatting | bytes 1024 | tf_op jit(solution)/shard_map/reshape | solution.py:405
  2.0 86.5 %gather_compute_scatter.1 = (bf16[16,4096]{1,0:T(8,128)(2,1)}, f32[128,1792]{1,0:T(8,128)}, f32[128,1792]{1,0:T(8,128)}) custom-call(bf16[1,16,4096]{2,1,0:T(8,128)(2,1)} %tok_hbm.1, bf16[1,4096,896]{2,1,0:T(8,128)(2,1)} %wg_hbm.1, bf16[1,4096,896]{2,1,0:T(8,128)(2,1)} %wu_hbm.1, bf16[1,512,896]{2,1,0:T(8,128)(2,1)} %dh_hbm.1, s32[1,128]{1,0:T(1,128)} %bitcast.3, ...), custom_call_target="tpu_custom_call" | custom-call | flops 16000000000 | bytes 18000000 | tf_op jit(solution)/shard_map/gather_compute_scatter/pallas_call | solution.py:356
  88.5 7.3 %update.1 = (bf16[1,16,4096]{2,1,0:T(8,128)(2,1)}, bf16[1,2,128,896]{3,2,1,0:T(8,128)(2,1)}, f32[2,128,896]{2,1,0:T(8,128)}, f32[2,128,896]{2,1,0:T(8,128)}, f32...) custom-call(bf16[16,4096]{1,0:T(8,128)(2,1)} %get-tuple-element.9.dtok, f32[128,1792]{1,0:T(8,128)} %get-tuple-element.10.grad, ...), custom_call_target="tpu_custom_call" | custom-call | tf_op jit(solution)/shard_map/update/pallas_call | solution.py:434

commit v2 on v0

v2 whole, which is shorter than its diff:
```python
import jax
import jax.numpy as jnp
from jax import lax
from jax.experimental import pallas as pl
from jax.experimental.pallas import tpu as pltpu
from jax.sharding import PartitionSpec as P

MESH = pl.DeviceIdType.MESH
BF = jnp.bfloat16
F32 = jnp.float32

D = 4096
HID = 896
W2 = 2 * HID
TOK = 512
OWN = 16
FRAG = 128
CHUNKS = ((0, 768), (768, 768), (1536, 768), (2304, 768), (3072, 512), (3584, 512))
NC = len(CHUNKS)
ND = 4
WIDE = 768
DW = 512
GATHER = (((0, 4), (0, 5)), ((0, 0), (0, 1)), ((0, 2), (0, 3)), ((1, 0), (1, 1)), ((1, 2), (1, 3)))
SCATTER = (((0, 0), (0, 1)), ((0, 2), (0, 3)), ((1, 0), (1, 1)), ((1, 2), (1, 3)), ((0, 4), (0, 5)))
T = len(GATHER)
HALF = TOK // 2
FACTOR = float(D) ** (-0.5)
NW = 4
WC = D // NW
MSG = 9
VMEM_GRANT = 55 * 2**20
DECAY = 1.0 - 0.02 * 0.1


def step_kernel(
    tok_hbm, wg_hbm, wu_hbm, dh_hbm, outer_hbm, mom_hbm, first_hbm, second_hbm, row_ref,
    dtokv, fragv, outerv, momv, firstv, secondv,
    wts, toks, acc, dcat, dhid, part, oh, oht, pick, rowp, rows_all,
    sb1, rb1, sb2, rb2, quart, sbx, rbx, sbd, rbd, own_sum,
    w_sem, l_sem, ag_s, ag_r, rs_s, rs_r, is_s, is_r,
):
    isl = lax.axis_index("island")
    f = lax.axis_index("fsdp")
    x = f // 16
    z = (f // 4) % 4
    y = f % 4
    xl = isl // 2
    core = isl % 2

    def at(xx, zz, yy):
        return (isl, xx * 16 + zz * 4 + yy)

    def up(m):
        return (m + 1) % 4

    def down(m):
        return (m + 3) % 4

    def opposite(m):
        return (m + 2) % 4

    ydev = (at(x, z, up(y)), at(x, z, down(y)), at(x, z, opposite(y)))
    zdev = (at(x, up(z), y), at(x, down(z), y), at(x, opposite(z), y))
    xdev = at(1 - x, z, y)
    isl_core = xl * 2 + (1 - core)
    isl_x = (1 - xl) * 2 + core
    isl_far = 3 - isl
    cdev = (isl_core, f)
    ldev = (isl_x, f)

    def ysl(m):
        return pl.ds(pl.multiple_of(m * OWN, OWN), OWN)

    own_copy = pltpu.make_async_copy(tok_hbm.at[0], toks.at[0, z, ysl(y), :], l_sem.at[0])
    own_copy.start()
    w_copies = []
    for p in range(NW):
        rows = pl.ds(p * WC, WC)
        pair = []
        for j, src in enumerate((wg_hbm, wu_hbm)):
            copy = pltpu.make_async_copy(
                src.at[0, rows, :], wts.at[rows, pl.ds(j * HID, HID)], w_sem.at[p, j]
            )
            copy.start()
            pair.append(copy)
        w_copies.append(pair)
    dh_copies = []
    for h, plane in ((0, x), (1, 1 - x)):
        rows = pl.ds(pl.multiple_of(plane * HALF, HALF), HALF)
        copy = pltpu.make_async_copy(dh_hbm.at[0, rows, :], dhid.at[h], l_sem.at[1 + h])
        copy.start()
        dh_copies.append(copy)
    state_copies = []
    for k, (src, dst) in enumerate(
        ((outer_hbm, outerv), (mom_hbm, momv), (first_hbm, firstv), (second_hbm, secondv))
    ):
        copy = pltpu.make_async_copy(src, dst, l_sem.at[3 + k])
        copy.start()
        state_copies.append(copy)

    barrier = pltpu.get_barrier_semaphore()
    greeted = (*ydev, *zdev, xdev, cdev, ldev)
    for dev in greeted:
        pl.semaphore_signal(barrier, inc=1, device_id=dev, device_id_type=MESH)

    spread = jnp.transpose(jnp.broadcast_to(row_ref[...], (FRAG, FRAG)))

    def hot(p, _):
        lo = pl.multiple_of(p * 128, 128)
        down_rows = lax.broadcasted_iota(jnp.int32, (128, FRAG), 0) + lo
        oh[pl.ds(lo, 128), :] = jnp.where(down_rows == row_ref[...], 1.0, 0.0).astype(BF)
        along = lax.broadcasted_iota(jnp.int32, (FRAG, 128), 1) + lo
        oht[:, pl.ds(lo, 128)] = jnp.where(along == spread, 1.0, 0.0).astype(BF)
        return 0

    pl.semaphore_wait(barrier, len(greeted))

    started = []

    def send(src, dst, ss, rs, dev):
        copy = pltpu.make_async_remote_copy(
            src_ref=src, dst_ref=dst, send_sem=ss, recv_sem=rs, device_id=dev, device_id_type=MESH
        )
        copy.start()
        started.append(copy)

    def arrived(ref, rs, ss):
        pltpu.make_async_remote_copy(
            src_ref=ref, dst_ref=ref, send_sem=ss, recv_sem=rs, device_id=xdev, device_id_type=MESH
        ).wait_recv()

    def cols_of(c, half=None):
        lo, w = CHUNKS[c]
        if half is None:
            return pl.ds(lo, w)
        return pl.ds(lo + half * (w // 2), w // 2)

    def axes(c):
        return ((y, ydev), (z, zdev)) if c % 2 == 0 else ((z, zdev), (y, ydev))

    def own_part(h, c, m):
        if c % 2 == 0:
            return toks.at[h, z, ysl(m), cols_of(c)]
        return toks.at[h, m, ysl(y), cols_of(c)]

    def ring_part(h, c, m, half=None):
        if c % 2 == 0:
            return toks.at[h, m, :, cols_of(c, half)]
        return toks.at[h, :, ysl(m), cols_of(c, half)]

    def spread_own(h, c):
        (m, dev), _ = axes(c)
        for j in range(3):
            piece = own_part(h, c, m)
            source = tok_hbm.at[0, :, cols_of(c)] if h == 0 else piece
            send(source, piece, ag_s.at[h, c, 1 + j], ag_r.at[h, c, 1 + j], dev[j])

    def spread_end(h, c):
        (m, _), _ = axes(c)
        for j, other in enumerate((down(m), up(m), opposite(m))):
            arrived(own_part(h, c, other), ag_r.at[h, c, 1 + j], ag_s.at[h, c, 1 + j])

    def ring_send(h, c):
        _, (m, dev) = axes(c)
        for j in range(2):
            piece = ring_part(h, c, m)
            send(piece, piece, ag_s.at[h, c, 5 + j], ag_r.at[h, c, 5 + j], dev[j])

    def ring_relay(h, c):
        _, (m, dev) = axes(c)
        for j, near in enumerate((down(m), up(m))):
            arrived(ring_part(h, c, near), ag_r.at[h, c, 5 + j], ag_s.at[h, c, 5 + j])
            piece = ring_part(h, c, near, j)
            send(piece, piece, ag_s.at[h, c, 7 + j], ag_r.at[h, c, 7 + j], dev[j])

    def ring_end(h, c):
        _, (m, _) = axes(c)
        for j in range(2):
            arrived(ring_part(h, c, opposite(m), j), ag_r.at[h, c, 7 + j], ag_s.at[h, c, 7 + j])

    for pair in GATHER[:3]:
        for h, c in pair:
            spread_own(h, c)
    for c in range(ND):
        send(
            tok_hbm.at[0, :, cols_of(c)], toks.at[1, z, ysl(y), cols_of(c)],
            ag_s.at[1, c, 0], ag_r.at[1, c, 0], xdev,
        )
    lax.fori_loop(0, D // 128, hot, 0)
    own_copy.wait()

    def spread_partner():
        for c in range(ND):
            arrived(toks.at[1, z, ysl(y), cols_of(c)], ag_r.at[1, c, 0], ag_s.at[1, c, 0])
            spread_own(1, c)

    def direct_send(c):
        send(
            toks.at[0, :, :, cols_of(c)], toks.at[1, :, :, cols_of(c)],
            ag_s.at[1, c, 0], ag_r.at[1, c, 0], xdev,
        )

    def direct_end(c):
        arrived(toks.at[1, :, :, cols_of(c)], ag_r.at[1, c, 0], ag_s.at[1, c, 0])

    def pick_rows(p):
        for copy in w_copies[p]:
            copy.wait()
        value = jnp.dot(
            oht[:, p * WC:(p + 1) * WC], wts[p * WC:(p + 1) * WC, :], preferred_element_type=F32
        )
        rowp[...] = value if p == 0 else value + rowp[...]

    def pick_all(lo, hi):
        for p in range(lo, hi):
            pick_rows(p)

    def share_rows():
        rows_all[isl] = rowp[...].astype(BF)
        send(rows_all.at[isl], rows_all.at[isl], is_s.at[0], is_r.at[0], cdev)
        send(rows_all.at[isl], rows_all.at[isl], is_s.at[1], is_r.at[1], ldev)

    def forward(h, c, start):
        lo, w = CHUNKS[c]
        hi = lo + w
        lhs = toks[h, :, :, lo:hi].reshape(HALF, w)
        value = jnp.dot(lhs, wts[lo:hi, :], preferred_element_type=F32)
        acc[h] = value if start else value + acc[h]
        value = jnp.dot(lhs, oh[lo:hi, :], preferred_element_type=F32)
        pick[h] = value if start else value + pick[h]

    def gated(h):
        dh_copies[h].wait()

        def body(r, _):
            rr = pl.ds(pl.multiple_of(r * 16, 16), 16)
            gate = acc[h, rr, 0:HID] * FACTOR
            upv = acc[h, rr, HID:W2] * FACTOR
            g = dhid[h, rr, :].astype(F32)
            s = jax.nn.sigmoid(gate)
            dcat[h, rr, 0:HID] = (g * upv * (s * (1.0 + gate * (1.0 - s)))).astype(BF)
            dcat[h, rr, HID:W2] = (g * (gate * s)).astype(BF)
            return 0

        lax.fori_loop(0, HALF // 16, body, 0)

    def backward(h, c):
        lo, w = CHUNKS[c]
        hi = lo + w
        value = lax.dot_general(
            dcat[h], wts[lo:hi, :], (((1,), (1,)), ((), ())), preferred_element_type=F32
        )
        if h == 1 and c >= ND:
            sbd[c - ND] = value.reshape(4, 64, w).astype(BF)
            send(sbd.at[c - ND], rbd.at[c - ND], rs_s.at[h, c, 8], rs_r.at[h, c, 8], xdev)
            return
        value = value.reshape(4, 64, w)
        if c >= ND:
            arrived(rbd.at[c - ND], rs_r.at[1, c, 8], rs_s.at[1, c, 8])
            value = value + rbd[c - ND].astype(F32)
        part[h, :, :, lo:hi] = value

    def scatter_axes(c):
        return ((z, zdev), (y, ydev)) if c % 2 == 0 else ((y, ydev), (z, zdev))

    def block1(h, c, m, half=None):
        if c % 2 == 0:
            return part[h, m, :, cols_of(c, half)]
        w = CHUNKS[c][1]
        return part[h, :, ysl(m), cols_of(c, half)].reshape(64, w if half is None else w // 2)

    def wide(c):
        return pl.ds(0, CHUNKS[c][1])

    def halves(c, j):
        w = CHUNKS[c][1] // 2
        return pl.ds(j * w, w)

    def far_out(h, c):
        (m, dev), _ = scatter_axes(c)
        sb1[h, c, 0, :, wide(c)] = block1(h, c, opposite(m)).astype(BF)
        for j in range(2):
            hs = halves(c, j)
            send(
                sb1.at[h, c, 0, :, hs], rb1.at[h, c, 0, :, hs],
                rs_s.at[h, c, j], rs_r.at[h, c, j], dev[j],
            )

    def near_out(h, c):
        (m, dev), _ = scatter_axes(c)
        for j, near in enumerate((up(m), down(m))):
            hs = halves(c, j)
            ot = halves(c, 1 - j)
            sb1[h, c, 1 + j, :, ot] = block1(h, c, near, 1 - j).astype(BF)
            arrived(rb1.at[h, c, 0, :, hs], rs_r.at[h, c, j], rs_s.at[h, c, j])
            sb1[h, c, 1 + j, :, hs] = (
                block1(h, c, near, j) + rb1[h, c, 0, :, hs].astype(F32)
            ).astype(BF)
            send(
                sb1.at[h, c, 1 + j, :, wide(c)], rb1.at[h, c, 1 + j, :, wide(c)],
                rs_s.at[h, c, 2 + j], rs_r.at[h, c, 2 + j], dev[j],
            )

    def ring_total(h, c):
        w = wide(c)
        (m, _), (m2, dev2) = scatter_axes(c)
        for j in range(2):
            arrived(rb1.at[h, c, 1 + j, :, w], rs_r.at[h, c, 2 + j], rs_s.at[h, c, 2 + j])
        value = block1(h, c, m) + (
            rb1[h, c, 1, :, w].astype(F32) + rb1[h, c, 2, :, w].astype(F32)
        )
        quart[h, c, :, :, w] = value.reshape(4, OWN, CHUNKS[c][1])
        for j, other in enumerate((up(m2), down(m2), opposite(m2))):
            sb2[h, c, j, :, w] = quart[h, c, other, :, w].astype(BF)
            send(
                sb2.at[h, c, j, :, w], rb2.at[h, c, j, :, w],
                rs_s.at[h, c, 4 + j], rs_r.at[h, c, 4 + j], dev2[j],
            )

    def plane_total(h, c):
        w = wide(c)
        _, (m2, _) = scatter_axes(c)
        for j in range(3):
            arrived(rb2.at[h, c, j, :, w], rs_r.at[h, c, 4 + j], rs_s.at[h, c, 4 + j])
        value = quart[h, c, m2, :, w] + (
            (rb2[h, c, 0, :, w].astype(F32) + rb2[h, c, 1, :, w].astype(F32))
            + rb2[h, c, 2, :, w].astype(F32)
        )
        if h == 1:
            sbx[c] = value.astype(BF)
            send(sbx.at[c], rbx.at[c], rs_s.at[h, c, 8], rs_r.at[h, c, 8], xdev)
        elif c < ND:
            own_sum[:, cols_of(c)] = value
        else:
            dtokv[:, cols_of(c)] = (value * FACTOR).astype(BF)

    def finish(c):
        arrived(rbx.at[c], rs_r.at[1, c, 8], rs_s.at[1, c, 8])
        value = own_sum[:, cols_of(c)] + rbx[c].astype(F32)
        dtokv[:, cols_of(c)] = (value * FACTOR).astype(BF)

    def gradient():
        pk = jnp.transpose(pick[...].reshape(TOK, FRAG)).astype(BF)
        acc[0, 0:FRAG, :] = (
            jnp.dot(pk, dcat[...].reshape(TOK, W2), preferred_element_type=F32) * FACTOR
        )

    def pass_rows():
        arrived(rows_all.at[isl_x], is_r.at[1], is_s.at[1])
        send(rows_all.at[isl_x], rows_all.at[isl_x], is_s.at[2], is_r.at[2], cdev)

    def optimize():
        arrived(rows_all.at[isl_core], is_r.at[0], is_s.at[0])
        arrived(rows_all.at[isl_far], is_r.at[2], is_s.at[2])
        for copy in state_copies:
            copy.wait()

        def body(i, _):
            rr = pl.ds(pl.multiple_of(i * 16, 16), 16)
            for j in range(2):
                cols = pl.ds(j * HID, HID)
                rsum = rows_all[0, rr, cols].astype(F32)
                for k in range(1, 4):
                    rsum = rsum + rows_all[k, rr, cols].astype(F32)
                outer = outerv[j, rr]
                g = acc[0, rr, cols]
                mean_delta = outer - rsum * 0.25
                mom = 0.9 * momv[j, rr] + mean_delta
                outer = outer - 0.7 * (mean_delta + 0.9 * mom)
                first = 0.9 * firstv[0, j, rr] + 0.1 * g
                second = 0.95 * secondv[0, j, rr] + 0.05 * (g * g)
                momv[j, rr] = mom
                outerv[j, rr] = outer
                firstv[0, j, rr] = first
                secondv[0, j, rr] = second
                fragv[0, j, rr] = (
                    outer * DECAY - 0.02 * first / (jnp.sqrt(second) + 1e-08)
                ).astype(BF)
            return 0

        lax.fori_loop(0, FRAG // 16, body, 0)

    for s in range(2 * T + 4):
        if s < T:
            for item in GATHER[s]:
                spread_end(*item)
                ring_send(*item)
        if s == 0:
            spread_partner()
            pick_all(0, NW // 2)
        if 0 <= s - 1 < T:
            for item in GATHER[s - 1]:
                ring_relay(*item)
        if s == 1:
            pick_all(NW // 2, NW)
        r = s - T
        if 0 <= r < T:
            if r == 2:
                for c in range(ND, NC):
                    backward(1, c)
            for item in SCATTER[r]:
                backward(*item)
                far_out(*item)
        if 0 <= r - 1 < T:
            for item in SCATTER[r - 1]:
                near_out(*item)
        if 0 <= r - 2 < T:
            for item in SCATTER[r - 2]:
                ring_total(*item)
        if 0 <= r - 3 < T:
            for item in SCATTER[r - 3]:
                plane_total(*item)
        if r == 0:
            share_rows()
        if r == 3:
            pass_rows()
            gradient()
        if r == 4:
            optimize()
        if 0 <= s - 2 < T:
            for h, c in GATHER[s - 2]:
                ring_end(h, c)
                if h == 0 and c >= ND:
                    direct_send(c)
                forward(h, c, s == 2 and c == ND or s == 5 and c == 0)
            if s == 4:
                gated(0)
            if s == 6:
                for c in range(ND, NC):
                    direct_end(c)
                    forward(1, c, False)
                gated(1)
    for c in range(ND):
        finish(c)

    for copy in started:
        copy.wait_send()


STATE = (
    jax.ShapeDtypeStruct((1, OWN, D), BF),
    jax.ShapeDtypeStruct((1, 2, FRAG, HID), BF),
    jax.ShapeDtypeStruct((2, FRAG, HID), F32),
    jax.ShapeDtypeStruct((2, FRAG, HID), F32),
    jax.ShapeDtypeStruct((1, 2, FRAG, HID), F32),
    jax.ShapeDtypeStruct((1, 2, FRAG, HID), F32),
)


def exchange(*args):
    any_spec = pl.BlockSpec(memory_space=pl.ANY)
    vmem = pl.BlockSpec(memory_space=pltpu.VMEM)
    dma = pltpu.SemaphoreType.DMA
    *arrays, fragment_rows = args
    return pl.pallas_call(
        step_kernel,
        out_shape=tuple(pltpu.VMEM(s.shape, s.dtype) for s in (jax.ShapeDtypeStruct((OWN, D), BF),) + STATE[1:]),
        in_specs=[any_spec] * 8 + [vmem],
        out_specs=(vmem,) * 6,
        scratch_shapes=[
            pltpu.VMEM((D, W2), BF),
            pltpu.VMEM((2, 4, 64, D), BF),
            pltpu.VMEM((2, HALF, W2), F32),
            pltpu.VMEM((2, HALF, W2), BF),
            pltpu.VMEM((2, HALF, HID), BF),
            pltpu.VMEM((2, 4, 64, D), F32),
            pltpu.VMEM((D, FRAG), BF),
            pltpu.VMEM((FRAG, D), BF),
            pltpu.VMEM((2, HALF, FRAG), F32),
            pltpu.VMEM((FRAG, W2), F32),
            pltpu.VMEM((4, FRAG, W2), BF),
            pltpu.VMEM((2, NC, 3, 64, WIDE), BF),
            pltpu.VMEM((2, NC, 3, 64, WIDE), BF),
            pltpu.VMEM((2, NC, 3, OWN, WIDE), BF),
            pltpu.VMEM((2, NC, 3, OWN, WIDE), BF),
            pltpu.VMEM((2, NC, 4, OWN, WIDE), F32),
            pltpu.VMEM((ND, OWN, WIDE), BF),
            pltpu.VMEM((ND, OWN, WIDE), BF),
            pltpu.VMEM((NC - ND, 4, 64, DW), BF),
            pltpu.VMEM((NC - ND, 4, 64, DW), BF),
            pltpu.VMEM((OWN, D), F32),
            dma((NW, 2)),
            dma((7,)),
            dma((2, NC, MSG)),
            dma((2, NC, MSG)),
            dma((2, NC, MSG)),
            dma((2, NC, MSG)),
            dma((3,)),
            dma((3,)),
        ],
        compiler_params=pltpu.CompilerParams(
            collective_id=0, has_side_effects=True, vmem_limit_bytes=VMEM_GRANT
        ),
        cost_estimate=pl.CostEstimate(
            flops=16 * 10**9, bytes_accessed=18 * 10**6, transcendentals=TOK * HID
        ),
        name="gather_compute_scatter",
    )(*arrays, fragment_rows.reshape(1, FRAG))


def copy_kernel(*refs):
    n = len(STATE)
    sems = refs[-1]
    copies = [
        pltpu.make_async_copy(refs[k], refs[n + k].at[0] if k == 0 else refs[n + k], sems.at[k])
        for k in range(n)
    ]
    for copy in copies:
        copy.start()
    for copy in copies:
        copy.wait()


def copy_out(results):
    n = len(STATE)
    return pl.pallas_call(
        copy_kernel,
        out_shape=STATE,
        in_specs=[pl.BlockSpec(memory_space=pltpu.VMEM)] * n,
        out_specs=(pl.BlockSpec(memory_space=pl.ANY),) * n,
        scratch_shapes=[pltpu.SemaphoreType.DMA((n,))],
        compiler_params=pltpu.CompilerParams(vmem_limit_bytes=8 * 2**20),
        name="copy_out",
    )(*results)


def per_device(
    tokens, w_gate, w_up, d_hidden, outer_rows, outer_momentum, adam_first, adam_second, fragment_rows
):
    return copy_out(
        exchange(
            tokens, w_gate, w_up, d_hidden, outer_rows, outer_momentum, adam_first, adam_second,
            fragment_rows,
        )
    )


def solution(mesh):
    return jax.shard_map(
        per_device,
        mesh=mesh,
        in_specs=(
            P("island", "fsdp", None),
            P("island", None, "fsdp"),
            P("island", None, "fsdp"),
            P("island", None, "fsdp"),
            P(None, None, "fsdp"),
            P(None, None, "fsdp"),
            P("island", None, None, "fsdp"),
            P("island", None, None, "fsdp"),
            P(),
        ),
        out_specs=(
            P("island", "fsdp", None),
            P("island", None, None, "fsdp"),
            P(None, None, "fsdp"),
            P(None, None, "fsdp"),
            P("island", None, None, "fsdp"),
            P("island", None, None, "fsdp"),
        ),
        check_vma=False,
    )
```

time: 341 us -> 74.3 us (0.22)
  waiting for transfers between devices: 259 us -> 0 us
  Pallas kernels: 0 us -> 73.3 us
  matrix products: 37.6 us -> 0 us
  local copies, waits for them, and re-layouts: 20.5 us -> 0 us
  between operations: 15.7 us -> 0.82 us
  other arithmetic: 7.4 us -> 0 us
    reduce_scatter x1 -> x0, waiting for transfers between devices: 184 us -> none  [per_device(): lax.psum_scatter(one_term(d_gate, gate_weights), 'fsdp', scatter_dimensio...]
    all_gather x1 -> x0, waiting for transfers between devices: 74 us -> none  [per_device(): gathered = lax.all_gather(tokens[0], 'fsdp', axis=0, tiled=True)]
    pallas_call x0 -> x2, Pallas kernels: none -> 73.3 us  [the longest x1 71.2 us: exchange(): pl.pallas_call(step_kernel, out_shape=tuple((pltpu.VMEM(s.shape, s.dtype)...]
    dot_general x6 -> x0, matrix products: 37.6 us -> none  [the longest x2 15.7 us: one_term(): lax.dot_general(cotangent, weights, contract, preferred_element_type=jnp....]
    gather x3 -> x0, local copies, waits for them, and re-layouts: 14 us -> none  [the longest x1 5.05 us: per_device(): jnp.take(gate_weights, fragment_rows, axis=0)]
    all_gather x1 -> x0, local copies, waits for them, and re-layouts: 6.47 us -> none  [per_device(): gathered = lax.all_gather(tokens[0], 'fsdp', axis=0, tiled=True)]
    convert_element_type x1 -> x0, other arithmetic: 3.97 us -> none  [per_device(): weights_new.astype(jnp.bfloat16)]
  transfers between devices with their start and end apart: 3 -> 0, of which waited for: 2 -> 0; matrix products, arithmetic and copies ran while one was open for 19% -> 0% of each run, Pallas kernels for 0% -> 0%
where the time goes in v2:
time: 74.3 us; the launch traced here: 74.1 us
  Pallas kernels  73.3 us (99%)
  between operations  0.82 us (1%)
    pallas_call x1, Pallas kernels, exchange(): pl.pallas_call(step_kernel, out_shape=tuple((pltpu.VMEM(s.shape, s.dtype)...  71.2 us
    pallas_call x1, Pallas kernels, copy_out(): pl.pallas_call(copy_kernel, out_shape=STATE, in_specs=[pl.BlockSpec(memor...  2.08 us

profile of v2, /device:TPU:0, one launch (start us, length us, event | category | flops | bytes accessed | tf_op | source)
XLA Modules:
  0.0 74.1 jit_solution(590458092686351792)
XLA Ops:
  0.6 71.2 %gather_compute_scatter.1 = (bf16[16,4096]{1,0:T(8,128)(2,1)S(1)}, bf16[1,2,128,896]{3,2,1,0:T(8,128)(2,1)S(1)}, f32[2,128,896]{2,1,0:T(8,128)S(1)}, f32[2,128,8...) custom-call(bf16[1,16,4096]{2,1,0:T(8,128)(2,1)} %tok_hbm.1, ...), custom_call_target="tpu_custom_call" | custom-call | flops 16000000000 | bytes 18000000 | tf_op jit(solution)/shard_map/gather_compute_scatter/pallas_call | solution.py:455
  71.9 2.1 %copy_out.1 = (bf16[1,16,4096]{2,1,0:T(8,128)(2,1)}, bf16[1,2,128,896]{3,2,1,0:T(8,128)(2,1)}, f32[2,128,896]{2,1,0:T(8,128)}, f32[2,128,896]{2,1,0:T(8,128)}, f...) custom-call(bf16[16,4096]{1,0:T(8,128)(2,1)S(1)} %get-tuple-element.12.refs_0_, ...), custom_call_target="tpu_custom_call" | custom-call | tf_op jit(solution)/shard_map/copy_out/pallas_call | solution.py:516

commit v3 on v2

--- a/solution.py
+++ b/solution.py
@@ -21,7 +21,6 @@
 WIDE = 768
 DW = 512
 GATHER = (((0, 4), (0, 5)), ((0, 0), (0, 1)), ((0, 2), (0, 3)), ((1, 0), (1, 1)), ((1, 2), (1, 3)))
-SCATTER = (((0, 0), (0, 1)), ((0, 2), (0, 3)), ((1, 0), (1, 1)), ((1, 2), (1, 3)), ((0, 4), (0, 5)))
 T = len(GATHER)
 HALF = TOK // 2
 FACTOR = float(D) ** (-0.5)
@@ -160,13 +159,25 @@
         for j, other in enumerate((down(m), up(m), opposite(m))):
             arrived(own_part(h, c, other), ag_r.at[h, c, 1 + j], ag_s.at[h, c, 1 + j])
 
+    def direct_send(c, k, m):
+        send(
+            ring_part(0, c, m), ring_part(1, c, m), ag_s.at[1, c, k], ag_r.at[1, c, k], xdev
+        )
+
+    def direct_end(c):
+        _, (m, _) = axes(c)
+        for k, other in enumerate((m, down(m), up(m), opposite(m))):
+            arrived(ring_part(1, c, other), ag_r.at[1, c, k], ag_s.at[1, c, k])
+
     def ring_send(h, c):
         _, (m, dev) = axes(c)
-        for j in range(2):
+        for j in range(3 if c >= ND else 2):
             piece = ring_part(h, c, m)
             send(piece, piece, ag_s.at[h, c, 5 + j], ag_r.at[h, c, 5 + j], dev[j])
 
     def ring_relay(h, c):
+        if c >= ND:
+            return
         _, (m, dev) = axes(c)
         for j, near in enumerate((down(m), up(m))):
             arrived(ring_part(h, c, near), ag_r.at[h, c, 5 + j], ag_s.at[h, c, 5 + j])
@@ -175,6 +186,11 @@
 
     def ring_end(h, c):
         _, (m, _) = axes(c)
+        if c >= ND:
+            for j, other in enumerate((down(m), up(m), opposite(m))):
+                arrived(ring_part(h, c, other), ag_r.at[h, c, 5 + j], ag_s.at[h, c, 5 + j])
+                direct_send(c, 1 + j, other)
+            return
         for j in range(2):
             arrived(ring_part(h, c, opposite(m), j), ag_r.at[h, c, 7 + j], ag_s.at[h, c, 7 + j])
 
@@ -194,15 +210,6 @@
             arrived(toks.at[1, z, ysl(y), cols_of(c)], ag_r.at[1, c, 0], ag_s.at[1, c, 0])
             spread_own(1, c)
 
-    def direct_send(c):
-        send(
-            toks.at[0, :, :, cols_of(c)], toks.at[1, :, :, cols_of(c)],
-            ag_s.at[1, c, 0], ag_r.at[1, c, 0], xdev,
-        )
-
-    def direct_end(c):
-        arrived(toks.at[1, :, :, cols_of(c)], ag_r.at[1, c, 0], ag_s.at[1, c, 0])
-
     def pick_rows(p):
         for copy in w_copies[p]:
             copy.wait()
@@ -220,7 +227,11 @@
         send(rows_all.at[isl], rows_all.at[isl], is_s.at[0], is_r.at[0], cdev)
         send(rows_all.at[isl], rows_all.at[isl], is_s.at[1], is_r.at[1], ldev)
 
-    def forward(h, c, start):
+    begun = set()
+
+    def forward(h, c):
+        start = h not in begun
+        begun.add(h)
         lo, w = CHUNKS[c]
         hi = lo + w
         lhs = toks[h, :, :, lo:hi].reshape(HALF, w)
@@ -254,11 +265,11 @@
             sbd[c - ND] = value.reshape(4, 64, w).astype(BF)
             send(sbd.at[c - ND], rbd.at[c - ND], rs_s.at[h, c, 8], rs_r.at[h, c, 8], xdev)
             return
-        value = value.reshape(4, 64, w)
-        if c >= ND:
-            arrived(rbd.at[c - ND], rs_r.at[1, c, 8], rs_s.at[1, c, 8])
-            value = value + rbd[c - ND].astype(F32)
-        part[h, :, :, lo:hi] = value
+        part[h, :, :, lo:hi] = value.reshape(4, 64, w)
+
+    def join(c):
+        arrived(rbd.at[c - ND], rs_r.at[1, c, 8], rs_s.at[1, c, 8])
+        part[0, :, :, cols_of(c)] = part[0, :, :, cols_of(c)] + rbd[c - ND].astype(F32)
 
     def scatter_axes(c):
         return ((z, zdev), (y, ydev)) if c % 2 == 0 else ((y, ydev), (z, zdev))
@@ -278,6 +289,15 @@
 
     def far_out(h, c):
         (m, dev), _ = scatter_axes(c)
+        if c >= ND:
+            w = wide(c)
+            for j, other in enumerate((up(m), down(m), opposite(m))):
+                sb1[h, c, j, :, w] = block1(h, c, other).astype(BF)
+                send(
+                    sb1.at[h, c, j, :, w], rb1.at[h, c, j, :, w],
+                    rs_s.at[h, c, j], rs_r.at[h, c, j], dev[j],
+                )
+            return
         sb1[h, c, 0, :, wide(c)] = block1(h, c, opposite(m)).astype(BF)
         for j in range(2):
             hs = halves(c, j)
@@ -304,11 +324,14 @@
     def ring_total(h, c):
         w = wide(c)
         (m, _), (m2, dev2) = scatter_axes(c)
-        for j in range(2):
-            arrived(rb1.at[h, c, 1 + j, :, w], rs_r.at[h, c, 2 + j], rs_s.at[h, c, 2 + j])
-        value = block1(h, c, m) + (
-            rb1[h, c, 1, :, w].astype(F32) + rb1[h, c, 2, :, w].astype(F32)
-        )
+        for j in range(3 if c >= ND else 2):
+            k = j if c >= ND else 1 + j
+            e = j if c >= ND else 2 + j
+            arrived(rb1.at[h, c, k, :, w], rs_r.at[h, c, e], rs_s.at[h, c, e])
+        value = rb1[h, c, 1, :, w].astype(F32) + rb1[h, c, 2, :, w].astype(F32)
+        if c >= ND:
+            value = value + rb1[h, c, 0, :, w].astype(F32)
+        value = block1(h, c, m) + value
         quart[h, c, :, :, w] = value.reshape(4, OWN, CHUNKS[c][1])
         for j, other in enumerate((up(m2), down(m2), opposite(m2))):
             sb2[h, c, j, :, w] = quart[h, c, other, :, w].astype(BF)
@@ -327,16 +350,16 @@
             + rb2[h, c, 2, :, w].astype(F32)
         )
         if h == 1:
-            sbx[c] = value.astype(BF)
-            send(sbx.at[c], rbx.at[c], rs_s.at[h, c, 8], rs_r.at[h, c, 8], xdev)
+            sbx[c, :, w] = value.astype(BF)
+            send(sbx.at[c, :, w], rbx.at[c, :, w], rs_s.at[h, c, 8], rs_r.at[h, c, 8], xdev)
         elif c < ND:
             own_sum[:, cols_of(c)] = value
         else:
             dtokv[:, cols_of(c)] = (value * FACTOR).astype(BF)
 
     def finish(c):
-        arrived(rbx.at[c], rs_r.at[1, c, 8], rs_s.at[1, c, 8])
-        value = own_sum[:, cols_of(c)] + rbx[c].astype(F32)
+        arrived(rbx.at[c, :, wide(c)], rs_r.at[1, c, 8], rs_s.at[1, c, 8])
+        value = own_sum[:, cols_of(c)] + rbx[c, :, wide(c)].astype(F32)
         dtokv[:, cols_of(c)] = (value * FACTOR).astype(BF)
 
     def gradient():
@@ -380,58 +403,89 @@
 
         lax.fori_loop(0, FRAG // 16, body, 0)
 
-    for s in range(2 * T + 4):
-        if s < T:
-            for item in GATHER[s]:
-                spread_end(*item)
-                ring_send(*item)
-        if s == 0:
-            spread_partner()
-            pick_all(0, NW // 2)
-        if 0 <= s - 1 < T:
-            for item in GATHER[s - 1]:
-                ring_relay(*item)
-        if s == 1:
-            pick_all(NW // 2, NW)
-        r = s - T
-        if 0 <= r < T:
-            if r == 2:
-                for c in range(ND, NC):
-                    backward(1, c)
-            for item in SCATTER[r]:
-                backward(*item)
-                far_out(*item)
-        if 0 <= r - 1 < T:
-            for item in SCATTER[r - 1]:
-                near_out(*item)
-        if 0 <= r - 2 < T:
-            for item in SCATTER[r - 2]:
-                ring_total(*item)
-        if 0 <= r - 3 < T:
-            for item in SCATTER[r - 3]:
-                plane_total(*item)
-        if r == 0:
-            share_rows()
-        if r == 3:
-            pass_rows()
-            gradient()
-        if r == 4:
-            optimize()
-        if 0 <= s - 2 < T:
-            for h, c in GATHER[s - 2]:
-                ring_end(h, c)
-                if h == 0 and c >= ND:
-                    direct_send(c)
-                forward(h, c, s == 2 and c == ND or s == 5 and c == 0)
-            if s == 4:
-                gated(0)
-            if s == 6:
-                for c in range(ND, NC):
-                    direct_end(c)
-                    forward(1, c, False)
-                gated(1)
+    def each(work, items):
+        for item in items:
+            work(*item)
+
+    o_direct, o_one, o_two, p_one, p_two = GATHER
+    direct = range(ND, NC)
+
+    def ring_start(items):
+        for item in items:
+            spread_end(*item)
+            ring_send(*item)
+
+    def multiply(items):
+        for item in items:
+            ring_end(*item)
+            forward(*item)
+
+    ring_start(o_direct)
+    for c in direct:
+        direct_send(c, 0, axes(c)[1][0])
+    pick_all(0, 1)
+    ring_start(o_one)
+    spread_partner()
+    ring_start(o_two)
+    pick_all(1, 2)
+    each(ring_end, o_direct)
+    pick_all(2, 4)
+    share_rows()
+    each(ring_relay, o_one)
+    each(forward, o_direct)
+    ring_start(p_one)
+    each(ring_relay, o_two)
+    ring_start(p_two)
+    multiply(o_one)
+    each(ring_relay, p_one)
+    multiply(o_two)
+    gated(0)
+
+    def multiply_back(items):
+        for item in items:
+            backward(*item)
+            far_out(*item)
+
+    each(ring_relay, p_two)
+    multiply_back(o_one)
+    multiply(p_one)
+    multiply_back(o_two)
+    each(near_out, o_one)
+    multiply(p_two)
+    for c in direct:
+        direct_end(c)
+        forward(1, c)
+    gated(1)
+    each(near_out, o_two)
+
+    for c in direct:
+        backward(1, c)
+    multiply_back(p_one)
+    each(ring_total, o_one)
+    multiply_back(p_two)
+    each(ring_total, o_two)
+    each(near_out, p_one)
+    pass_rows()
+    each(plane_total, o_one)
+    each(backward, o_direct)
+    each(near_out, p_two)
+    join(ND)
+    far_out(0, ND)
+    each(plane_total, o_two)
+    each(ring_total, p_one)
+    gradient()
+    each(ring_total, p_two)
+    join(ND + 1)
+    far_out(0, ND + 1)
+    each(plane_total, p_one)
+    optimize()
+    ring_total(0, ND)
+    each(plane_total, p_two)
+    ring_total(0, ND + 1)
+    plane_total(0, ND)
     for c in range(ND):
         finish(c)
+    plane_total(0, ND + 1)
 
     for copy in started:
         copy.wait_send()

time: 74.3 us -> 73.4 us (0.988)
  Pallas kernels: 73.3 us -> 72.5 us
    pallas_call x1, Pallas kernels: 71.2 us -> 70.4 us  [exchange(): pl.pallas_call(step_kernel, out_shape=tuple((pltpu.VMEM(s.shape, s.dtype)...]
where the time goes in v3:
time: 73.4 us; the launch traced here: 73.3 us
  Pallas kernels  72.5 us (99%)
  between operations  0.82 us (1%)
    pallas_call x1, Pallas kernels, exchange(): pl.pallas_call(step_kernel, out_shape=tuple((pltpu.VMEM(s.shape, s.dtype)...  70.4 us
    pallas_call x1, Pallas kernels, copy_out(): pl.pallas_call(copy_kernel, out_shape=STATE, in_specs=[pl.BlockSpec(memor...  2.08 us

profile of v3, /device:TPU:0, one launch (start us, length us, event | category | flops | bytes accessed | tf_op | source)
XLA Modules:
  0.0 73.3 jit_solution(14025091486979085429)
XLA Ops:
  0.6 70.4 %gather_compute_scatter.1 = (bf16[16,4096]{1,0:T(8,128)(2,1)S(1)}, bf16[1,2,128,896]{3,2,1,0:T(8,128)(2,1)S(1)}, f32[2,128,896]{2,1,0:T(8,128)S(1)}, f32[2,128,8...) custom-call(bf16[1,16,4096]{2,1,0:T(8,128)(2,1)} %tok_hbm.1, ...), custom_call_target="tpu_custom_call" | custom-call | flops 16000000000 | bytes 18000000 | tf_op jit(solution)/shard_map/gather_compute_scatter/pallas_call | solution.py:509
  71.0 2.1 %copy_out.1 = (bf16[1,16,4096]{2,1,0:T(8,128)(2,1)}, bf16[1,2,128,896]{3,2,1,0:T(8,128)(2,1)}, f32[2,128,896]{2,1,0:T(8,128)}, f32[2,128,896]{2,1,0:T(8,128)}, f...) custom-call(bf16[16,4096]{1,0:T(8,128)(2,1)S(1)} %get-tuple-element.12.refs_0_, ...), custom_call_target="tpu_custom_call" | custom-call | tf_op jit(solution)/shard_map/copy_out/pallas_call | solution.py:570

commit v4 on v3

--- a/solution.py
+++ b/solution.py
@@ -237,8 +237,9 @@
         lhs = toks[h, :, :, lo:hi].reshape(HALF, w)
         value = jnp.dot(lhs, wts[lo:hi, :], preferred_element_type=F32)
         acc[h] = value if start else value + acc[h]
-        value = jnp.dot(lhs, oh[lo:hi, :], preferred_element_type=F32)
-        pick[h] = value if start else value + pick[h]
+
+    def pick_columns(h):
+        pick[h] = jnp.dot(toks[h].reshape(HALF, D), oh[...], preferred_element_type=F32)
 
     def gated(h):
         dh_copies[h].wait()
@@ -467,6 +468,8 @@
     each(near_out, p_one)
     pass_rows()
     each(plane_total, o_one)
+    pick_columns(0)
+    pick_columns(1)
     each(backward, o_direct)
     each(near_out, p_two)
     join(ND)

time: 73.4 us -> 74.4 us (1.014)
  Pallas kernels: 72.5 us -> 73.5 us
    pallas_call x1, Pallas kernels: 70.4 us -> 71.4 us  [exchange(): pl.pallas_call(step_kernel, out_shape=tuple((pltpu.VMEM(s.shape, s.dtype)...]
where the time goes in v4:
time: 74.4 us; the launch traced here: 74.3 us
  Pallas kernels  73.5 us (99%)
  between operations  0.82 us (1%)
    pallas_call x1, Pallas kernels, exchange(): pl.pallas_call(step_kernel, out_shape=tuple((pltpu.VMEM(s.shape, s.dtype)...  71.4 us
    pallas_call x1, Pallas kernels, copy_out(): pl.pallas_call(copy_kernel, out_shape=STATE, in_specs=[pl.BlockSpec(memor...  2.08 us

profile of v4, /device:TPU:0, one launch (start us, length us, event | category | flops | bytes accessed | tf_op | source)
XLA Modules:
  0.0 74.3 jit_solution(14953437681710581261)
XLA Ops:
  0.6 71.4 %gather_compute_scatter.1 = (bf16[16,4096]{1,0:T(8,128)(2,1)S(1)}, bf16[1,2,128,896]{3,2,1,0:T(8,128)(2,1)S(1)}, f32[2,128,896]{2,1,0:T(8,128)S(1)}, f32[2,128,8...) custom-call(bf16[1,16,4096]{2,1,0:T(8,128)(2,1)} %tok_hbm.1, ...), custom_call_target="tpu_custom_call" | custom-call | flops 16000000000 | bytes 18000000 | tf_op jit(solution)/shard_map/gather_compute_scatter/pallas_call | solution.py:512
  72.1 2.1 %copy_out.1 = (bf16[1,16,4096]{2,1,0:T(8,128)(2,1)}, bf16[1,2,128,896]{3,2,1,0:T(8,128)(2,1)}, f32[2,128,896]{2,1,0:T(8,128)}, f32[2,128,896]{2,1,0:T(8,128)}, f...) custom-call(bf16[16,4096]{1,0:T(8,128)(2,1)S(1)} %get-tuple-element.12.refs_0_, ...), custom_call_target="tpu_custom_call" | custom-call | tf_op jit(solution)/shard_map/copy_out/pallas_call | solution.py:573
